TPU v7x, 256 devices: a whole 4x4x8 slice. The times are simulated.
256 devices in a mesh: row: 16 (over z, y_hi), col: 16 (over y_lo, x, core).
Axes of the slice: x: 4, y: 4 (y_hi: 2, y_lo: 2; y = y_hi * 2 + y_lo), z: 8, core: 2. Of those that a mesh axis runs over, the one named last changes fastest.
Arguments:
- adjoint_in: bfloat16 [2, 16, 2560, 1536], P(None, None, 'col', 'row'), may hold values from -6 to 6
- solve_inverse: bfloat16 [16, 1536, 1536], P('row'), may hold values from -0.4 to 1.6
- gradient_fields: bfloat16 [4, 16, 1536, 3840], P(None, 'row', 'col'), may hold values from -5 to 5
Outputs:
- adjoint_out: float32 [2, 16, 2560, 1536], P(None, None, 'col', 'row')
All inputs are finite; a program needn't handle non-finite values.
Results may differ from a plain program's by a relative error of at most 0.0032.
Values may be sent and summed in bfloat16 or wider, within the bound.
A program may use at most 64 MiB of HBM per device.

v0:
```python
import math

import jax
import jax.numpy as jnp
from jax import lax
from jax.sharding import PartitionSpec as P

NY = 1536
NZ = 3840
KZ = 2560


step_weight = 0.5


def cheb_build(length_y):
    row_index = lax.broadcasted_iota(jnp.int32, (length_y, length_y), 0)
    col_index = lax.broadcasted_iota(jnp.int32, (length_y, length_y), 1)
    residue = row_index * col_index % (2 * (length_y - 1))
    angles = residue.astype(jnp.float32) * jnp.float32(math.pi / (length_y - 1))
    return (jnp.cos(angles) * jnp.float32(math.sqrt(2.0 / length_y))).astype(jnp.bfloat16)


def fourier_build(modes, points_z):
    mode_index = lax.broadcasted_iota(jnp.int32, (modes, points_z), 0)
    point_index = lax.broadcasted_iota(jnp.int32, (modes, points_z), 1)
    wavenumber = (mode_index + 1) // 2
    residue = wavenumber * point_index % points_z
    angles = residue.astype(jnp.float32) * jnp.float32(2.0 * math.pi / points_z)
    angles = angles - (mode_index % 2).astype(jnp.float32) * jnp.float32(math.pi / 2.0)
    return (jnp.cos(angles) * jnp.float32(math.sqrt(2.0 / points_z))).astype(jnp.bfloat16)


def on_device(adjoint_in, solve_inverse, gradient_fields):
    cheb_table = cheb_build(NY)
    fourier = fourier_build(KZ, NZ)
    gathered = lax.all_to_all(adjoint_in, "row", split_axis=1, concat_axis=3, tiled=True)
    solved = jnp.einsum(
        "cpkj,pji->cpki", gathered, solve_inverse, preferred_element_type=jnp.float32
    )
    points = jnp.einsum(
        "cpki,iy->cpky", solved.astype(jnp.bfloat16), cheb_table, preferred_element_type=jnp.float32
    ).astype(jnp.bfloat16)
    physical = jnp.einsum(
        "cpky,kz->cpyz",
        lax.all_to_all(points, "col", split_axis=3, concat_axis=2, tiled=True),
        fourier,
        preferred_element_type=jnp.float32,
    )
    grads = gradient_fields.astype(jnp.float32)
    force_u = grads[0] * physical[0] + grads[2] * physical[1]
    force_v = grads[1] * physical[0] + grads[3] * physical[1]
    forcing = jnp.stack([force_u, force_v]).astype(jnp.bfloat16)
    analysed = jnp.einsum(
        "cpyz,kz->cpky", forcing, fourier, preferred_element_type=jnp.float32
    ).astype(jnp.bfloat16)
    lines = lax.all_to_all(analysed, "col", split_axis=2, concat_axis=3, tiled=True)
    correction = jnp.einsum("cpky,yi->cpki", lines, cheb_table, preferred_element_type=jnp.float32)
    updated = solved + jnp.float32(step_weight) * correction
    return lax.all_to_all(updated, "row", split_axis=3, concat_axis=1, tiled=True)


def solution(mesh):
    return jax.shard_map(
        on_device,
        mesh=mesh,
        in_specs=(P(None, None, "col", "row"), P("row", None, None), P(None, "row", "col", None)),
        out_specs=P(None, None, "col", "row"),
        check_vma=False,
    )
```

profile of v0, /device:TPU:1, one launch (start us, length us, event | category | flops | bytes accessed | tf_op | source)
XLA Modules:
  0.0 602.8 jit_solution(7068242476837874936)
XLA Ops:
  0.0 1.4 copy.14
  1.4 46.3 %all_to_all.63 = bf16[2,16,160,96]{3,2,0,1:T(8,128)(2,1)S(1)} all-to-all(bf16[2,16,160,96]{3,2,0,1:T(8,128)(2,1)S(1)} %copy.14), channel_id=1, replica_groups=mesh['row'=16,'col'=16] {'row'}, dimensions={1} | all-to-all | bytes 1966080 | tf_op jit(solution)/shard_map/all_to_all | solution.py:37
  47.7 0.8 copy.15
  48.5 1.5 reshape.45
  50.0 4.0 fusion.44
  54.0 0.0 copy-start
  54.1 1.3 copy-done
  55.3 38.1 %fusion.56 = bf16[2,1,160,1536]{3,2,0,1:T(8,128)(2,1)S(1)} fusion(f32[2,1,160,1536]{3,2,0,1:T(8,128)S(1)} %fusion.44), kind=kOutput, calls=%fused_computation.42 | convolution fusion | flops 1536884736 | bytes 2949120 | tf_op jit(solution)/shard_map/cpki,iy->cpky/dot_general | solution.py:41
  93.5 2.9 copy.16
  96.3 6.8 %all-to-all-start.1 = ((bf16[2,1,160,1536]{2,0,1,3:T(2,128)(2,1)}), bf16[2,1,160,1536]{2,0,1,3:T(2,128)(2,1)S(1)}, u32[]{:S(2)}, u32[]{:S(2)}) async-start(bf16[2,1,160,1536]{2,0,1,3:T(2,128)(2,1)} %copy.16), calls=%async_computation.1 | async-start | bytes 3145728 | tf_op jit(solution)/shard_map/all_to_all | solution.py:46
  103.1 4.9 convert_element_type.53
  108.0 16.6 %all-to-all-done.1 = bf16[2,1,160,1536]{2,0,1,3:T(2,128)(2,1)S(1)} async-done(((bf16[2,1,160,1536]{2,0,1,3:T(2,128)(2,1)}), bf16[2,1,160,1536]{2,0,1,3:T(2,128)(2,1)S(1)}, u32[]{:S(2)}, u32[]{:S(2)}) %all-to-all-start.1) | async-done | bytes 983072 | tf_op jit(solution)/shard_map/all_to_all | solution.py:46
  124.6 0.0 slice-start
  124.6 3.9 copy.17
  128.5 0.0 slice-start.1
  128.5 157.5 %fusion.12 = f32[2,96,3840]{2,1,0:T(8,128)S(1)} fusion(bf16[2,2560,96]{2,1,0:T(8,128)(2,1)} %bitcast.125, s32[2560]{0:T(1024)S(1)} %get-tuple-element.8, s32[2560]{0:T(1024)S(1)} %get-tuple-element.9, s32[2560]{0:T(1024)S(1)} %get-tuple-element.7, s32[2560]{0:T(1024)S(1)} %get-tuple-element.10, pred[2560]{0:T(1024)(128)(4,1)S(1)} %get-tuple-element.12, ...), kind=kOutput, calls=%fused_computation.14 | convolution fusion | flops 3932160000 | bytes 3978240 | tf_op jit(solution)/shard_map/cpky,kz->cpyz/dot_general | solution.py:44
  286.1 0.0 slice-done
  286.1 0.0 slice-done.1
  286.1 0.5 fusion.65
  286.6 0.1 fusion.123
  286.8 164.4 %fusion.38 = bf16[2,1,2560,96]{2,3,0,1:T(8,128)(2,1)S(1)} fusion(s32[2560]{0:T(1024)S(1)} %get-tuple-element.8, s32[2560]{0:T(1024)S(1)} %get-tuple-element.9, s32[2560]{0:T(1024)S(1)} %get-tuple-element.7, s32[2560]{0:T(1024)S(1)} %get-tuple-element.10, pred[2560]{0:T(1024)(128)(4,1)S(1)} %get-tuple-element.12, pred[2560]{0:T(1024)(128)(4,1)S(1)} %get-tuple-element.11, ...), kind=kOutput, calls=%fused_computation.36 | convolution fusion | flops 3932651520 | bytes 2503680 | tf_op jit(solution)/shard_map/cpyz,kz->cpky/dot_general | solution.py:54
  451.2 1.0 copy.19
  452.2 22.1 %all_to_all.64 = bf16[2,1,2560,96]{3,0,1,2:T(2,128)(2,1)S(1)} all-to-all(bf16[2,1,2560,96]{3,0,1,2:T(2,128)(2,1)S(1)} %copy.19), channel_id=1, replica_groups=mesh['row'=16,'col'=16] {'col'}, dimensions={2} | all-to-all | bytes 1966080 | tf_op jit(solution)/shard_map/all_to_all | solution.py:57
  474.4 0.2 copy.20
  474.5 0.5 copy.21
  475.1 1.5 reshape.48
  476.5 39.8 %fusion.50 = f32[2,1,160,1536]{3,2,0,1:T(8,128)} fusion(f32[2,1,160,1536]{3,2,0,1:T(8,128)} %copy-done, bf16[2,160,1536]{2,1,0:T(8,128)(2,1)S(1)} %reshape.48), kind=kOutput, calls=%fused_computation.40 | convolution fusion | flops 1536884736 | bytes 4915200 | tf_op jit(solution)/shard_map/cpky,yi->cpki/dot_general | solution.py:58
  516.3 3.9 copy.22
  520.2 76.7 %all_to_all.65 = f32[2,1,160,1536]{2,0,1,3:T(2,128)} all-to-all(f32[2,1,160,1536]{2,0,1,3:T(2,128)S(1)} %copy.22), channel_id=1, replica_groups=mesh['row'=16,'col'=16] {'row'}, dimensions={3} | all-to-all | bytes 3932160 | tf_op jit(solution)/shard_map/all_to_all | solution.py:60
  597.0 5.7 copy.23
  (4 shorter events, 0.0 us)
Async XLA Ops:
  54.0 1.3 copy-start
  96.3 28.3 %all-to-all-start.1 = ((bf16[2,1,160,1536]{2,0,1,3:T(2,128)(2,1)}), bf16[2,1,160,1536]{2,0,1,3:T(2,128)(2,1)S(1)}, u32[]{:S(2)}, u32[]{:S(2)}) async-start(bf16[2,1,160,1536]{2,0,1,3:T(2,128)(2,1)} %copy.16), calls=%async_computation.1 | async-start | bytes 3145728 | tf_op jit(solution)/shard_map/all_to_all | solution.py:46
  124.6 161.5 %slice-start = ((s8[5898240]{0:T(1024)(128)(4,1)}), s8[1703936]{0:T(1024)(128)(4,1)S(1)}, s32[]{:S(2)}) async-start(s8[5898240]{0:T(1024)(128)(4,1)} %bitcast.119), calls=%async_computation.4 | async-start | bytes 3407872
  128.5 157.5 %slice-start.1 = ((s8[5898240]{0:T(1024)(128)(4,1)}), s8[4194304]{0:T(1024)(128)(4,1)S(1)}, s32[]{:S(2)}) async-start(s8[5898240]{0:T(1024)(128)(4,1)} %bitcast.119), calls=%async_computation.5 | async-start | bytes 8388608
where the time goes:
time: 607 us; the launch traced here: 603 us
  matrix products  404 us (67%)
  blocking collectives  145 us (24%)
  local copies, waits for them, and re-layouts  24.6 us (4%)
  waiting for transfers between devices  16.6 us (3%)
  starting transfers between devices  6.78 us (1%)
    dot_general x1, matrix products, on_device(): jnp.einsum('cpyz,kz->cpky', forcing, fourier, preferred_element_type=jnp....  164 us
    dot_general x1, matrix products, on_device(): jnp.einsum('cpky,kz->cpyz', lax.all_to_all(points, 'col', split_axis=3, c...  158 us
    all_to_all x1, blocking collectives, on_device(): lax.all_to_all(updated, 'row', split_axis=3, concat_axis=1, tiled=True)  76.7 us
    all_to_all x1, blocking collectives, on_device(): lax.all_to_all(adjoint_in, 'row', split_axis=1, concat_axis=3, tiled=True)  46.3 us
    dot_general x1, matrix products, on_device(): jnp.einsum('cpky,yi->cpki', lines, cheb_table, preferred_element_type=jnp...  39.8 us
    dot_general x1, matrix products, on_device(): jnp.einsum('cpki,iy->cpky', solved.astype(jnp.bfloat16), cheb_table, pref...  38.1 us
    all_to_all x1, blocking collectives, on_device(): lax.all_to_all(analysed, 'col', split_axis=2, concat_axis=3, tiled=True)  22.1 us
    all_to_all x1, waiting for transfers between devices, on_device(): lax.all_to_all(points, 'col', split_axis=3, concat_axis=2, tiled=True)  16.6 us
  transfers between devices with their start and end apart: 1, of which 1 were waited for; matrix products, arithmetic and copies ran while one was open for 1% of the time, Pallas kernels for 0%

commit v1 on v0

v1 whole, which is shorter than its diff:
```python
import math

import jax
import jax.numpy as jnp
import ml_dtypes
import numpy as np
from jax import lax
from jax.sharding import PartitionSpec as P

NY = 1536
NZ = 3840
KZ = 2560


step_weight = 0.5


def cheb_build(length_y):
    index = np.arange(length_y, dtype=np.int64)
    residue = index[:, None] * index[None, :] % (2 * (length_y - 1))
    table = np.cos(np.arange(2 * (length_y - 1)) * (math.pi / (length_y - 1))) * math.sqrt(2.0 / length_y)
    return table.astype(np.float32).astype(ml_dtypes.bfloat16)[residue]


def fourier_build(modes, points_z):
    k = np.arange(modes, dtype=np.int64)
    residue = ((k + 1) // 2)[:, None] * np.arange(points_z, dtype=np.int64)[None, :] % points_z
    angles = np.arange(points_z) * (2.0 * math.pi / points_z)
    scale = math.sqrt(2.0 / points_z)
    both = np.stack([np.cos(angles), np.sin(angles)]) * scale
    both = both.astype(np.float32).astype(ml_dtypes.bfloat16)
    return both[(k % 2)[:, None], residue]


def on_device(adjoint_in, solve_inverse, gradient_fields):
    cheb_table = jnp.asarray(cheb_build(NY))
    fourier = jnp.asarray(fourier_build(KZ, NZ))
    gathered = lax.all_to_all(adjoint_in, "row", split_axis=1, concat_axis=3, tiled=True)
    solved = jnp.einsum(
        "cpkj,pji->cpki", gathered, solve_inverse, preferred_element_type=jnp.float32
    )
    points = jnp.einsum(
        "cpki,iy->cpky", solved.astype(jnp.bfloat16), cheb_table, preferred_element_type=jnp.float32
    ).astype(jnp.bfloat16)
    physical = jnp.einsum(
        "cpky,kz->cpyz",
        lax.all_to_all(points, "col", split_axis=3, concat_axis=2, tiled=True),
        fourier,
        preferred_element_type=jnp.float32,
    )
    grads = gradient_fields.astype(jnp.float32)
    force_u = grads[0] * physical[0] + grads[2] * physical[1]
    force_v = grads[1] * physical[0] + grads[3] * physical[1]
    forcing = jnp.stack([force_u, force_v]).astype(jnp.bfloat16)
    analysed = jnp.einsum(
        "cpyz,kz->cpky", forcing, fourier, preferred_element_type=jnp.float32
    ).astype(jnp.bfloat16)
    lines = lax.all_to_all(analysed, "col", split_axis=2, concat_axis=3, tiled=True)
    correction = jnp.einsum("cpky,yi->cpki", lines, cheb_table, preferred_element_type=jnp.float32)
    updated = solved + jnp.float32(step_weight) * correction
    sent = updated.astype(jnp.bfloat16)
    return lax.all_to_all(sent, "row", split_axis=3, concat_axis=1, tiled=True).astype(jnp.float32)


def solution(mesh):
    return jax.shard_map(
        on_device,
        mesh=mesh,
        in_specs=(P(None, None, "col", "row"), P("row", None, None), P(None, "row", "col", None)),
        out_specs=P(None, None, "col", "row"),
        check_vma=False,
    )
```

time: 607 us -> 195 us (0.32)
  matrix products: 404 us -> 32.4 us
  blocking collectives: 145 us -> 111 us
    dot_general x1, matrix products: 164 us -> 10.7 us  [on_device(): jnp.einsum('cpyz,kz->cpky', forcing, fourier, preferred_element_type=jnp....]
    dot_general x1, matrix products: 158 us -> 9.02 us  [on_device(): jnp.einsum('cpky,kz->cpyz', lax.all_to_all(points, 'col', split_axis=3, c...]
    dot_general x1, matrix products: 39.8 us -> 4.67 us  [on_device(): jnp.einsum('cpky,yi->cpki', lines, cheb_table, preferred_element_type=jnp...]
    all_to_all x1, blocking collectives: 76.7 us -> 42.2 us  [on_device(): lax.all_to_all(sent, 'row', split_axis=3, concat_axis=1, tiled=True)]
    dot_general x1, matrix products: 38.1 us -> 4.02 us  [on_device(): jnp.einsum('cpki,iy->cpky', solved.astype(jnp.bfloat16), cheb_table, pref...]
  transfers between devices with their start and end apart: 1 -> 1, of which waited for: 1 -> 1; matrix products, arithmetic and copies ran while one was open for 1% -> 3% of each run, Pallas kernels for 0% -> 0%
where the time goes in v1:
time: 195 us; the launch traced here: 194 us
  blocking collectives  111 us (57%)
  matrix products  32.4 us (17%)
  local copies, waits for them, and re-layouts  21.9 us (11%)
  waiting for transfers between devices  16.6 us (9%)
  starting transfers between devices  6.78 us (3%)
  other arithmetic  5.34 us (3%)
    all_to_all x1, blocking collectives, on_device(): lax.all_to_all(adjoint_in, 'row', split_axis=1, concat_axis=3, tiled=True)  46.3 us
    all_to_all x1, blocking collectives, on_device(): lax.all_to_all(sent, 'row', split_axis=3, concat_axis=1, tiled=True)  42.2 us
    all_to_all x1, blocking collectives, on_device(): lax.all_to_all(analysed, 'col', split_axis=2, concat_axis=3, tiled=True)  22.1 us
    all_to_all x1, waiting for transfers between devices, on_device(): lax.all_to_all(points, 'col', split_axis=3, concat_axis=2, tiled=True)  16.6 us
    dot_general x1, matrix products, on_device(): jnp.einsum('cpyz,kz->cpky', forcing, fourier, preferred_element_type=jnp....  10.7 us
    dot_general x1, matrix products, on_device(): jnp.einsum('cpky,kz->cpyz', lax.all_to_all(points, 'col', split_axis=3, c...  9.02 us
    all_to_all x1, starting transfers between devices, on_device(): lax.all_to_all(points, 'col', split_axis=3, concat_axis=2, tiled=True)  6.78 us
    convert_element_type x1, other arithmetic, on_device(): grads = gradient_fields.astype(jnp.float32)  4.85 us
  transfers between devices with their start and end apart: 1, of which 1 were waited for; matrix products, arithmetic and copies ran while one was open for 3% of the time, Pallas kernels for 0%

profile of v1, /device:TPU:1, one launch (start us, length us, event | category | flops | bytes accessed | tf_op | source)
XLA Modules:
  0.0 193.8 jit_solution(17622390506048857823)
XLA Ops:
  0.0 1.4 copy.15
  1.4 46.3 %all_to_all.54 = bf16[2,16,160,96]{3,2,0,1:T(8,128)(2,1)S(1)} all-to-all(bf16[2,16,160,96]{3,2,0,1:T(8,128)(2,1)S(1)} %copy.15), channel_id=1, replica_groups=mesh['row'=16,'col'=16] {'row'}, dimensions={1} | all-to-all | bytes 1966080 | tf_op jit(solution)/shard_map/all_to_all | solution.py:38
  47.7 0.8 copy.16
  48.5 1.5 reshape.49
  50.0 4.0 %fusion.3 = f32[2,1,160,1536]{3,2,0,1:T(8,128)S(1)} fusion(bf16[2,160,1536]{2,1,0:T(8,128)(2,1)S(1)} %reshape.49, bf16[1,1536,1536]{2,1,0:T(8,128)(2,1)} %param.6), kind=kOutput, calls=%fused_computation.5 | convolution fusion | flops 1509949440 | bytes 7667712 | tf_op jit(solution)/shard_map/cpkj,pji->cpki/dot_general | solution.py:39
  54.0 0.0 copy-start
  54.1 1.3 copy-done
  55.3 4.0 %fusion.9 = bf16[2,1,160,1536]{3,2,0,1:T(8,128)(2,1)S(1)} fusion(bf16[1536,1536,1]{1,0,2:T(8,128)(2,1)} %constant.13, f32[2,1,160,1536]{3,2,0,1:T(8,128)S(1)} %fusion.3), kind=kOutput, calls=%fused_computation.10 | convolution fusion | flops 1510932480 | bytes 7667712 | tf_op jit(solution)/shard_map/cpki,iy->cpky/dot_general | solution.py:42
  59.3 2.9 %copy.17 = bf16[2,1,160,1536]{2,0,1,3:T(2,128)(2,1)} copy(bf16[2,1,160,1536]{3,2,0,1:T(8,128)(2,1)S(1)} %fusion.9) | data formatting | bytes 1966080 | tf_op jit(solution)/shard_map/convert_element_type | solution.py:44
  62.2 6.8 %all-to-all-start.1 = ((bf16[2,1,160,1536]{2,0,1,3:T(2,128)(2,1)}), bf16[2,1,160,1536]{2,0,1,3:T(2,128)(2,1)S(1)}, u32[]{:S(2)}, u32[]{:S(2)}) async-start(bf16[2,1,160,1536]{2,0,1,3:T(2,128)(2,1)} %copy.17), calls=%async_computation.1 | async-start | bytes 3145728 | tf_op jit(solution)/shard_map/all_to_all | solution.py:47
  69.0 4.9 %convert_element_type.43 = f32[4,1,96,3840]{3,2,1,0:T(8,128)} convert(bf16[4,1,96,3840]{3,2,1,0:T(8,128)(2,1)} %param.7) | non-fusion elementwise | flops 1474560 | bytes 8847360 | tf_op jit(solution)/shard_map/convert_element_type | solution.py:51
  73.8 16.6 %all-to-all-done.1 = bf16[2,1,160,1536]{2,0,1,3:T(2,128)(2,1)S(1)} async-done(((bf16[2,1,160,1536]{2,0,1,3:T(2,128)(2,1)}), bf16[2,1,160,1536]{2,0,1,3:T(2,128)(2,1)S(1)}, u32[]{:S(2)}, u32[]{:S(2)}) %all-to-all-start.1) | async-done | bytes 983072 | tf_op jit(solution)/shard_map/all_to_all | solution.py:47
  90.5 2.8 %copy.18 = bf16[2,1,160,1536]{3,2,0,1:T(8,128)(2,1)} copy(bf16[2,1,160,1536]{2,0,1,3:T(2,128)(2,1)S(1)} %all-to-all-done.1) | data formatting | bytes 1966080 | tf_op jit(solution)/shard_map/all_to_all | solution.py:47
  93.3 0.0 slice-start
  93.3 2.6 %reshape.53 = bf16[2,2560,96]{2,1,0:T(8,128)(2,1)S(1)} reshape(bf16[2,1,160,1536]{3,2,0,1:T(8,128)(2,1)} %copy.18) | data formatting | bytes 1966080 | tf_op jit(solution)/shard_map/cpky,kz->cpyz/dot_general | solution.py:45
  96.0 0.0 slice-start.1
  96.0 9.0 %fusion.20 = f32[2,96,3840]{2,1,0:T(8,128)S(1)} fusion(bf16[2,2560,96]{2,1,0:T(8,128)(2,1)S(1)} %reshape.53, bf16[2560,3840,1]{1,0,2:T(8,128)(2,1)} %constant.14), kind=kOutput, calls=%fused_computation.27 | convolution fusion | flops 3774873600 | bytes 23592960 | tf_op jit(solution)/shard_map/cpky,kz->cpyz/dot_general | solution.py:45
  105.0 0.0 slice-done
  105.0 0.0 slice-done.1
  105.0 0.5 fusion.16
  105.5 10.7 %fusion.2 = bf16[2,1,2560,96]{2,3,0,1:T(8,128)(2,1)S(1)} fusion(bf16[2560,3840,1]{1,0,2:T(8,128)(2,1)} %constant.15, bf16[1,96,3840]{2,1,0:T(8,128)(2,1)S(1)} %get-tuple-element.6, bf16[1,96,3840]{2,1,0:T(8,128)(2,1)S(1)} %get-tuple-element.5), kind=kOutput, calls=%fused_computation.3 | convolution fusion | flops 3776102400 | bytes 22118400 | tf_op jit(solution)/shard_map/cpyz,kz->cpky/dot_general | solution.py:55
  116.2 1.0 copy.20
  117.2 22.1 %all_to_all.55 = bf16[2,1,2560,96]{3,0,1,2:T(2,128)(2,1)S(1)} all-to-all(bf16[2,1,2560,96]{3,0,1,2:T(2,128)(2,1)S(1)} %copy.20), channel_id=1, replica_groups=mesh['row'=16,'col'=16] {'col'}, dimensions={2} | all-to-all | bytes 1966080 | tf_op jit(solution)/shard_map/all_to_all | solution.py:58
  139.4 0.2 copy.21
  139.6 0.5 copy.22
  140.1 1.5 reshape.52
  141.6 4.7 %fusion.8 = bf16[2,1,160,1536]{3,2,0,1:T(8,128)(2,1)S(1)} fusion(f32[2,1,160,1536]{3,2,0,1:T(8,128)} %copy-done, bf16[2,160,1536]{2,1,0:T(8,128)(2,1)S(1)} %reshape.52, bf16[1536,1536,1]{1,0,2:T(8,128)(2,1)} %constant.13), kind=kOutput, calls=%fused_computation.8 | convolution fusion | flops 1511424000 | bytes 8650752 | tf_op jit(solution)/shard_map/cpky,yi->cpki/dot_general | solution.py:59
  146.2 1.2 copy.23
  147.5 42.2 %all_to_all.56 = bf16[2,1,160,1536]{2,0,1,3:T(2,128)(2,1)S(1)} all-to-all(bf16[2,1,160,1536]{2,0,1,3:T(2,128)(2,1)S(1)} %copy.23), channel_id=1, replica_groups=mesh['row'=16,'col'=16] {'row'}, dimensions={3} | all-to-all | bytes 1966080 | tf_op jit(solution)/shard_map/all_to_all | solution.py:62
  189.7 4.1 %copy.24 = f32[2,1,160,16,96]{4,2,3,0,1:T(8,128)} copy(bf16[2,1,160,16,96]{2,0,4,3,1:T(2,128)(2,1)S(1)} %bitcast.90) | data formatting | bytes 2949120 | tf_op jit(solution)/shard_map/convert_element_type | solution.py:62
  (1 shorter events, 0.0 us)
Async XLA Ops:
  54.0 1.3 copy-start
  62.2 28.3 %all-to-all-start.1 = ((bf16[2,1,160,1536]{2,0,1,3:T(2,128)(2,1)}), bf16[2,1,160,1536]{2,0,1,3:T(2,128)(2,1)S(1)}, u32[]{:S(2)}, u32[]{:S(2)}) async-start(bf16[2,1,160,1536]{2,0,1,3:T(2,128)(2,1)} %copy.17), calls=%async_computation.1 | async-start | bytes 3145728 | tf_op jit(solution)/shard_map/all_to_all | solution.py:47
  93.3 11.7 %slice-start = ((s8[5898240]{0:T(1024)(128)(4,1)}), s8[1703936]{0:T(1024)(128)(4,1)S(1)}, s32[]{:S(2)}) async-start(s8[5898240]{0:T(1024)(128)(4,1)} %bitcast.88), calls=%async_computation.4 | async-start | bytes 3407872
  96.0 9.1 %slice-start.1 = ((s8[5898240]{0:T(1024)(128)(4,1)}), s8[4194304]{0:T(1024)(128)(4,1)S(1)}, s32[]{:S(2)}) async-start(s8[5898240]{0:T(1024)(128)(4,1)} %bitcast.88), calls=%async_computation.5 | async-start | bytes 8388608

commit v2 on v1

v2 whole, which is shorter than its diff:
```python
import functools
import math

import jax
import jax.numpy as jnp
import ml_dtypes
import numpy as np
from jax import lax
from jax.experimental import pallas as pl
from jax.experimental.pallas import tpu as pltpu
from jax.sharding import PartitionSpec as P

NY = 1536
NZ = 3840
KZ = 2560

step_weight = 0.5

LANES = 128
SHARE = 96
CHUNKS = (32, 32, 32, 32, 32)
VMEM_LIMIT = 60 * 1024 * 1024
MESH = pl.DeviceIdType.MESH
NT = (((1,), (1,)), ((), ()))


def cheb_build(length_y):
    index = np.arange(length_y, dtype=np.int64)
    residue = index[:, None] * index[None, :] % (2 * (length_y - 1))
    table = np.cos(np.arange(2 * (length_y - 1)) * (math.pi / (length_y - 1))) * math.sqrt(2.0 / length_y)
    table = table.astype(np.float32).astype(ml_dtypes.bfloat16)[residue]
    table = table.reshape(length_y // SHARE, SHARE, length_y)
    table = np.pad(table, ((0, 0), (0, LANES - SHARE), (0, 0)))
    return table.reshape(-1, length_y)


def fourier_build(modes, points_z, devices, chunks):
    local = np.arange(modes, dtype=np.int64).reshape(devices, modes // devices)
    starts = np.cumsum((0,) + chunks)
    k = np.concatenate([local[:, a:b].reshape(-1) for a, b in zip(starts[:-1], starts[1:])])
    residue = ((k + 1) // 2)[:, None] * np.arange(points_z, dtype=np.int64)[None, :] % points_z
    angles = np.arange(points_z) * (2.0 * math.pi / points_z)
    both = np.stack([np.cos(angles), np.sin(angles)]) * math.sqrt(2.0 / points_z)
    both = both.astype(np.float32).astype(ml_dtypes.bfloat16)
    return both[(k % 2)[:, None], residue]


def lane_of(rows):
    return lax.broadcasted_iota(jnp.int32, (rows, LANES), 1)


def pack(first, second):
    rows = first.shape[0]
    half = rows // 2
    lane = lane_of(rows)
    turned = pltpu.roll(second, 96, 1)
    top = jnp.where(lane < 96, first, turned)
    low = jnp.where(lane[:half] < 64, turned[:half], pltpu.roll(turned[half:], 64, 1))
    return jnp.concatenate([top, low], axis=0).astype(jnp.bfloat16)


def unpack(block, rows):
    block = block.astype(jnp.float32)
    top, low = block[:rows], block[rows:]
    full = jnp.concatenate([low, pltpu.roll(low, 64, 1)], axis=0)
    second = pltpu.roll(jnp.where(lane_of(rows) < 64, full, top), 32, 1)
    return top, second


def kernel(
    chunks, adj, inv, grads, cheb, four, out,
    adj_v, inv_v, grads_v, cheb_v, four_v,
    send_a, recv_a, send_b, recv_b, send_c, recv_c, send_d, recv_d,
    lhs, solved, rounded, line, turned, phys, force, out_v,
    load_sem, send_sem, recv_sem, out_sem,
):
    f32, bf16 = jnp.float32, jnp.bfloat16
    groups = adj.shape[1]
    length_y = inv.shape[1]
    points_z = four.shape[1]
    row, col = lax.axis_index("row"), lax.axis_index("col")
    starts = [sum(chunks[:q]) for q in range(len(chunks))]
    count = len(chunks)
    tile = 256 if length_y % 256 == 0 else 128

    def local(source, target, sem):
        copy = pltpu.make_async_copy(source, target, sem)
        copy.start()
        return copy

    adj_loads = [
        local(adj.at[:, :, pl.ds(starts[q], chunks[q])], adj_v.at[:, :, pl.ds(starts[q], chunks[q])], load_sem.at[q])
        for q in range(count)
    ]
    for s in range(groups):
        local(inv.at[0, pl.ds(s * SHARE, SHARE)], inv_v.at[pl.ds(s * LANES, SHARE)], load_sem.at[count])
    cheb_load = local(cheb, cheb_v, load_sem.at[count + 1])
    four_loads = []
    for q in range(count):
        part = pl.ds(groups * starts[q], groups * chunks[q])
        four_loads.append(local(four.at[part], four_v.at[part], load_sem.at[count + 3 + q]))
    grads_load = local(grads, grads_v, load_sem.at[count + 2])

    barrier = pltpu.get_barrier_semaphore()

    def greet(t, carry):
        pl.semaphore_signal(barrier, inc=1, device_id={"row": lax.rem(row + t, groups)}, device_id_type=MESH)
        pl.semaphore_signal(barrier, inc=1, device_id={"col": lax.rem(col + t, groups)}, device_id_type=MESH)
        return carry

    lax.fori_loop(1, groups, greet, 0)

    def packed(q):
        return pl.ds(starts[q] * 3 // 2, chunks[q] * 3 // 2)

    def exchange_one(axis, phase, q, t, send, recv):
        me = row if axis == "row" else col
        peer = lax.rem(me + t, groups)
        pltpu.make_async_remote_copy(
            src_ref=send.at[peer, packed(q)],
            dst_ref=recv.at[me, packed(q)],
            send_sem=send_sem.at[phase, q],
            recv_sem=recv_sem.at[phase, q],
            device_id={axis: peer},
            device_id_type=MESH,
        ).start()

    def exchange(axis, phase, q, send, recv):
        def one(t, carry):
            exchange_one(axis, phase, q, t, send, recv)
            return carry

        lax.fori_loop(1, groups, one, 0)
        me = row if axis == "row" else col
        recv[me, packed(q)] = send[me, packed(q)]

    def arrived(phase, q, recv):
        every = recv.at[pl.ds(0, groups - 1), packed(q)]
        pltpu.make_async_copy(every, every, recv_sem.at[phase, q]).wait()

    def sent(phase, q, send):
        every = send.at[pl.ds(0, groups - 1), packed(q)]
        pltpu.make_async_copy(every, every, send_sem.at[phase, q]).wait()

    for s in range(groups):
        inv_v[s * LANES + SHARE : (s + 1) * LANES, :] = jnp.zeros((LANES - SHARE, length_y), bf16)
    for c in range(2):
        force[c * LANES + SHARE : (c + 1) * LANES, :] = jnp.zeros((LANES - SHARE, points_z), bf16)

    for q in range(count):
        size, at = chunks[q], starts[q]
        adj_loads[q].wait()

        def spread(p, carry, size=size, at=at, q=q):
            blank = jnp.zeros((size, LANES - SHARE), f32)
            parts = [
                jnp.concatenate([adj_v[c, p, pl.ds(at, size), :].astype(f32), blank], axis=1) for c in range(2)
            ]
            send_a[p, packed(q)] = pack(*parts)
            return carry

        lax.fori_loop(0, groups, spread, 0)
        if q == 0:
            pl.semaphore_wait(barrier, 2 * (groups - 1))
        exchange("row", 0, q, send_a, recv_a)

    def gather(q, recv):
        size = chunks[q]

        def one(s, carry):
            first, second = unpack(recv[s, packed(q)], size)
            at = pl.ds(pl.multiple_of(s * LANES, LANES), LANES)
            lhs[0:size, at] = first.astype(bf16)
            lhs[size : 2 * size, at] = second.astype(bf16)
            return carry

        lax.fori_loop(0, groups, one, 0)

    def to_points(q):
        size, at = chunks[q], starts[q]
        arrived(0, q, recv_a)
        gather(q, recv_a)
        if q == 0:
            whole = inv_v.at[pl.ds(0, groups * SHARE)]
            pltpu.make_async_copy(whole, whole, load_sem.at[count]).wait()

        def solve(n, carry):
            cols = pl.ds(pl.multiple_of(n * tile, tile), tile)
            value = jnp.dot(lhs[0 : 2 * size, :], inv_v[:, cols], preferred_element_type=f32)
            solved[2 * at : 2 * (at + size), cols] = value
            rounded[0 : 2 * size, cols] = value.astype(bf16)
            return carry

        lax.fori_loop(0, length_y // tile, solve, 0)
        if q == 0:
            cheb_load.wait()

        def evaluate(n, carry):
            rows = pl.ds(pl.multiple_of(n * 256, 256), 256)
            value = lax.dot_general(rounded[0 : 2 * size, :], cheb_v[rows, :], NT, preferred_element_type=f32)
            for j in range(2):
                part = slice(j * LANES, (j + 1) * LANES)
                send_b[2 * n + j, packed(q)] = pack(value[:size, part], value[size:, part])
            return carry

        lax.fori_loop(0, groups // 2, evaluate, 0)
        exchange("col", 1, q, send_b, recv_b)

    def to_physical(q):
        size, at = chunks[q], starts[q]
        depth = groups * size
        arrived(1, q, recv_b)

        def one(s, carry):
            first, second = unpack(recv_b[s, packed(q)], size)
            rows = pl.ds(pl.multiple_of(s * size, size), size)
            line[0, rows, :] = first
            line[1, rows, :] = second
            return carry

        lax.fori_loop(0, groups, one, 0)

        def turn(b, carry):
            rows = pl.ds(pl.multiple_of(b * LANES, LANES), LANES)
            for c in range(2):
                turned[c * LANES : (c + 1) * LANES, rows] = line[c, rows, :].T.astype(bf16)
            return carry

        lax.fori_loop(0, depth // LANES, turn, 0)
        four_loads[q].wait()
        if q == count - 1:
            grads_load.wait()

        def synthesise(n, carry):
            cols = pl.ds(pl.multiple_of(n * 256, 256), 256)
            value = jnp.dot(
                turned[:, 0:depth], four_v[groups * at : groups * (at + size), cols], preferred_element_type=f32
            )
            if q > 0:
                value = value + phys[:, cols]
            if q < count - 1:
                phys[:, cols] = value
            else:
                first, second = value[0:SHARE], value[LANES : LANES + SHARE]
                g = [grads_v[i, 0, :, cols].astype(f32) for i in range(4)]
                force[0:SHARE, cols] = (g[0] * first + g[2] * second).astype(bf16)
                force[LANES : LANES + SHARE, cols] = (g[1] * first + g[3] * second).astype(bf16)
            return carry

        lax.fori_loop(0, points_z // 256, synthesise, 0)

    def analyse(q):
        size, at = chunks[q], starts[q]
        several = max(1, min(groups, 256 // size))

        def one(n, carry):
            rows = pl.ds(pl.multiple_of(groups * at + n * (several * size), 16), several * size)
            value = lax.dot_general(four_v[rows, :], force[...], NT, preferred_element_type=f32)
            for j in range(several):
                part = value[j * size : (j + 1) * size]
                send_c[n * several + j, packed(q)] = pack(part[:, :LANES], part[:, LANES:])
            return carry

        lax.fori_loop(0, groups // several, one, 0)
        exchange("col", 2, q, send_c, recv_c)

    def update(q):
        size, at = chunks[q], starts[q]
        arrived(2, q, recv_c)
        gather(q, recv_c)

        def one(n, carry):
            cols = pl.ds(pl.multiple_of(n * 384, 384), 384)
            value = jnp.dot(lhs[0 : 2 * size, :], cheb_v[:, cols], preferred_element_type=f32)
            value = solved[2 * at : 2 * (at + size), cols] + f32(step_weight) * value
            lane = lane_of(size)
            shares = []
            for c in range(2):
                t = [value[c * size : (c + 1) * size, i * LANES : (i + 1) * LANES] for i in range(3)]
                shares.append([
                    t[0],
                    jnp.where(lane < 32, pltpu.roll(t[0], 32, 1), pltpu.roll(t[1], 32, 1)),
                    jnp.where(lane < 64, pltpu.roll(t[1], 64, 1), pltpu.roll(t[2], 64, 1)),
                    pltpu.roll(t[2], 96, 1),
                ])
            for j in range(4):
                send_d[4 * n + j, packed(q)] = pack(shares[0][j], shares[1][j])
            return carry

        lax.fori_loop(0, groups // 4, one, 0)
        exchange("row", 3, q, send_d, recv_d)

    def finish(q):
        size, at = chunks[q], starts[q]
        arrived(3, q, recv_d)

        def one(s, carry):
            for c, part in enumerate(unpack(recv_d[s, packed(q)], size)):
                out_v[c, s, pl.ds(at, size), :] = part[:, :SHARE].astype(bf16)
            return carry

        lax.fori_loop(0, groups, one, 0)
        return local(out_v.at[:, :, pl.ds(at, size)], out.at[:, :, pl.ds(at, size)], out_sem.at[q])

    for q in range(count):
        to_points(q)
        if q > 0:
            to_physical(q - 1)
    to_physical(count - 1)
    for q in range(count):
        analyse(q)
    for q in range(count):
        update(q)
    writes = [finish(q) for q in range(count)]
    for q in range(count):
        for phase, send in enumerate((send_a, send_b, send_c, send_d)):
            sent(phase, q, send)
        writes[q].wait()


def on_device(groups, chunks, adjoint_in, solve_inverse, gradient_fields):
    local_modes = adjoint_in.shape[2]
    length_y = solve_inverse.shape[1]
    points_z = gradient_fields.shape[3]
    cheb = jnp.asarray(cheb_build(length_y))
    four = jnp.asarray(fourier_build(local_modes * groups, points_z, groups, chunks))
    f32, bf16 = jnp.float32, jnp.bfloat16
    most = max(chunks)
    count = len(chunks)
    mail = pltpu.VMEM((groups, local_modes * 3 // 2, LANES), bf16)
    result = pl.pallas_call(
        functools.partial(kernel, chunks),
        out_shape=jax.ShapeDtypeStruct(adjoint_in.shape, bf16),
        in_specs=[pl.BlockSpec(memory_space=pl.ANY)] * 5,
        out_specs=pl.BlockSpec(memory_space=pl.ANY),
        scratch_shapes=[
            pltpu.VMEM(adjoint_in.shape, bf16),
            pltpu.VMEM(cheb.shape, bf16),
            pltpu.VMEM(gradient_fields.shape, bf16),
            pltpu.VMEM(cheb.shape, bf16),
            pltpu.VMEM(four.shape, bf16),
            *[mail] * 8,
            pltpu.VMEM((2 * most, groups * LANES), bf16),
            pltpu.VMEM((2 * local_modes, length_y), f32),
            pltpu.VMEM((2 * most, length_y), bf16),
            pltpu.VMEM((2, groups * most, LANES), f32),
            pltpu.VMEM((2 * LANES, groups * most), bf16),
            pltpu.VMEM((2 * LANES, points_z), f32),
            pltpu.VMEM((2 * LANES, points_z), bf16),
            pltpu.VMEM(adjoint_in.shape, bf16),
            pltpu.SemaphoreType.DMA((2 * count + 3,)),
            pltpu.SemaphoreType.DMA((4, count)),
            pltpu.SemaphoreType.DMA((4, count)),
            pltpu.SemaphoreType.DMA((count,)),
        ],
        compiler_params=pltpu.CompilerParams(
            collective_id=0, has_side_effects=True, vmem_limit_bytes=VMEM_LIMIT
        ),
        cost_estimate=pl.CostEstimate(flops=12_000_000_000, bytes_accessed=40_000_000, transcendentals=0),
    )(adjoint_in, solve_inverse, gradient_fields, cheb, four)
    return result.astype(f32)


def solution(mesh):
    groups = mesh.shape["row"]
    return jax.shard_map(
        functools.partial(on_device, groups, CHUNKS),
        mesh=mesh,
        in_specs=(P(None, None, "col", "row"), P("row", None, None), P(None, "row", "col", None)),
        out_specs=P(None, None, "col", "row"),
        check_vma=False,
    )
```

time: 195 us -> 140 us (0.72)
  Pallas kernels: 0 us -> 137 us
  blocking collectives: 111 us -> 0 us
  matrix products: 32.4 us -> 0 us
  local copies, waits for them, and re-layouts: 21.9 us -> 0 us
  waiting for transfers between devices: 16.6 us -> 0 us
  starting transfers between devices: 6.78 us -> 0 us
  other arithmetic: 5.34 us -> 3.12 us
    pallas_call x0 -> x1, Pallas kernels: none -> 137 us  [on_device(): pl.pallas_call(functools.partial(kernel, chunks), out_shape=jax.ShapeDtyp...]
    all_to_all x3 -> x0, blocking collectives: 111 us -> none  [the longest x1 46.3 us: on_device(): lax.all_to_all(adjoint_in, 'row', split_axis=1, concat_axis=3, tiled=True)]
    dot_general x5 -> x0, matrix products: 32.4 us -> none  [the longest x1 10.7 us: on_device(): jnp.einsum('cpyz,kz->cpky', forcing, fourier, preferred_element_type=jnp....]
    all_to_all x1 -> x0, waiting for transfers between devices: 16.6 us -> none  [on_device(): lax.all_to_all(points, 'col', split_axis=3, concat_axis=2, tiled=True)]
    convert_element_type x4 -> x0, local copies, waits for them, and re-layouts: 9.2 us -> none  [the longest x1 4.09 us: on_device(): lax.all_to_all(sent, 'row', split_axis=3, concat_axis=1, tiled=True)]
    all_to_all x1 -> x0, starting transfers between devices: 6.78 us -> none  [on_device(): lax.all_to_all(points, 'col', split_axis=3, concat_axis=2, tiled=True)]
    all_to_all x4 -> x0, local copies, waits for them, and re-layouts: 4.36 us -> none  [the longest x1 2.83 us: on_device(): lax.all_to_all(points, 'col', split_axis=3, concat_axis=2, tiled=True)]
    another operation x2 -> x0, local copies, waits for them, and re-layouts: 2.94 us -> none
  transfers between devices with their start and end apart: 1 -> 0, of which waited for: 1 -> 0; matrix products, arithmetic and copies ran while one was open for 3% -> 0% of each run, Pallas kernels for 0% -> 0%
where the time goes in v2:
time: 140 us
  Pallas kernels  137 us (98%)
  other arithmetic  3.12 us (2%)
    pallas_call x1, Pallas kernels, on_device(): pl.pallas_call(functools.partial(kernel, chunks), out_shape=jax.ShapeDtyp...  137 us
    convert_element_type x1, other arithmetic, on_device(): return result.astype(f32)  3.12 us

profile of v2, /device:TPU:1, one launch (start us, length us, event | category | flops | bytes accessed | tf_op | source)
XLA Modules:
  0.0 140.1 jit_solution(9397360851389404203)
XLA Ops:
  0.0 137.0 %shard_map.55 = bf16[2,16,160,96]{3,2,1,0:T(8,128)(2,1)} custom-call(bf16[2,16,160,96]{3,2,1,0:T(8,128)(2,1)} %adj.1, bf16[1,1536,1536]{2,1,0:T(8,128)(2,1)} %inv.1, bf16[4,1,96,3840]{3,2,1,0:T(8,128)(2,1)} %grads.1, bf16[2048,1536]{1,0:T(8,128)(2,1)} %constant.4.clone.cheb, bf16[2560,3840]{1,0:T(8,128)(2,1)} %constant.5.clone.four), custom_call_target="tpu_custom_call" | custom-call | flops 12000000000 | bytes 40000000 | tf_op jit(solution)/shard_map/pallas_call | solution.py:331
  137.0 3.1 %convert_element_type.3 = f32[2,16,160,96]{3,2,1,0:T(8,128)} convert(bf16[2,16,160,96]{3,2,1,0:T(8,128)(2,1)} %shard_map.55) | non-fusion elementwise | flops 491520 | bytes 2949120 | tf_op jit(solution)/shard_map/convert_element_type | solution.py:361

commit v3 on v2

v3 whole, which is shorter than its diff:
```python
import functools
import math

import jax
import jax.numpy as jnp
import ml_dtypes
import numpy as np
from jax import lax
from jax.experimental import pallas as pl
from jax.experimental.pallas import tpu as pltpu
from jax.sharding import PartitionSpec as P

NY = 1536
NZ = 3840
KZ = 2560

step_weight = 0.5

LANES = 128
BLOCK = 256
BATCH = 16
SHARE = 96
CHUNKS = (64, 64, 32)
SOLVE_TILE = 768
POST = 4
WIDTH = 640
VMEM_LIMIT = 60 * 1024 * 1024
MESH = pl.DeviceIdType.MESH
NT = (((1,), (1,)), ((), ()))


def cheb_build(length_y):
    index = np.arange(length_y, dtype=np.int64)
    residue = index[:, None] * index[None, :] % (2 * (length_y - 1))
    table = np.cos(np.arange(2 * (length_y - 1)) * (math.pi / (length_y - 1))) * math.sqrt(2.0 / length_y)
    return table.astype(np.float32).astype(ml_dtypes.bfloat16)[residue]


def parity_order():
    n = np.arange(BLOCK)
    odd = (n + 1) // 2 % 2
    return np.concatenate([n[odd == 0], n[odd == 1]])


def parity_build():
    forward = np.zeros((BLOCK, BLOCK), np.float32)
    forward[parity_order(), np.arange(BLOCK)] = 1.0
    return forward.astype(ml_dtypes.bfloat16)


def fourier_build(modes, points_z, devices, chunks):
    local = np.arange(modes, dtype=np.int64).reshape(devices, modes // devices)
    starts = np.cumsum((0,) + chunks)
    k = np.concatenate([local[:, a:b].reshape(-1) for a, b in zip(starts[:-1], starts[1:])])
    k = k.reshape(-1, BLOCK)[:, parity_order()].reshape(-1, 2, BLOCK // 2)
    k = k.transpose(1, 0, 2).reshape(2, modes // 2, 1)
    residue = (k + 1) // 2 * np.arange(points_z // 2, dtype=np.int64) % points_z
    angles = np.arange(points_z) * (2.0 * math.pi / points_z)
    both = np.stack([np.cos(angles), np.sin(angles)]) * math.sqrt(2.0 / points_z)
    both = both.astype(np.float32).astype(ml_dtypes.bfloat16)
    return both[k % 2, residue]


def below(shape, limit):
    return lax.broadcasted_iota(jnp.int16, shape, len(shape) - 1) < jnp.int16(limit)


def pack(first, second):
    half, last = first.shape[-2] // 2, first.ndim - 1
    turned = pltpu.roll(second, 96, last)
    top = jnp.where(below(first.shape, 96), first, turned)
    upper, lower = turned[..., :half, :], turned[..., half:, :]
    low = jnp.where(below(upper.shape, 64), upper, pltpu.roll(lower, 64, last))
    return jnp.concatenate([top, low], axis=last - 1)


def unpack(block):
    rows, last = block.shape[-2] * 2 // 3, block.ndim - 1
    top, low = block[..., :rows, :], block[..., rows:, :]
    full = jnp.concatenate([low, pltpu.roll(low, 64, last)], axis=last - 1)
    second = pltpu.roll(jnp.where(below(top.shape, 64), full, top), 32, last)
    return top, second


def spread_lanes(tiles):
    shape = tiles[0].shape
    middle = [pltpu.roll(t, 32, 1) for t in tiles[:2]], [pltpu.roll(t, 64, 1) for t in tiles[1:]]
    return [
        tiles[0],
        jnp.where(below(shape, 32), *middle[0]),
        jnp.where(below(shape, 64), *middle[1]),
        pltpu.roll(tiles[2], 96, 1),
    ]


def close_lanes(parts):
    shape = parts[0].shape
    turned = [pltpu.roll(p, shift, 1) for p, shift in zip(parts[1:], (96, 64, 32))]
    return [
        jnp.where(below(shape, 96), parts[0], turned[0]),
        jnp.where(below(shape, 64), turned[0], turned[1]),
        jnp.where(below(shape, 32), turned[1], turned[2]),
    ]


def kernel(
    chunks, adj, inv, grads, cheb, four, parity, out,
    adj_v, inv_v, grads_v, cheb_v, four_v, parity_v,
    send_a, recv_a, send_b, recv_b, send_c, recv_c, send_d, recv_d,
    lhs, solved, rounded, turned, sorted_v, phys, force, out_v,
    load_sem, send_sem, recv_sem, out_sem,
):
    f32, bf16 = jnp.float32, jnp.bfloat16
    groups = adj.shape[1]
    length_y = inv.shape[1]
    half_z = four.shape[2]
    row, col = lax.axis_index("row"), lax.axis_index("col")
    starts = [sum(chunks[:q]) for q in range(len(chunks))]
    count = len(chunks)
    tile = math.gcd(length_y, SOLVE_TILE)
    quads = min(POST, groups // 4)

    def local(source, target, sem):
        copy = pltpu.make_async_copy(source, target, sem)
        copy.start()
        return copy

    adj_loads = [
        local(adj.at[:, :, pl.ds(starts[q], chunks[q])], adj_v.at[:, :, pl.ds(starts[q], chunks[q])], load_sem.at[q])
        for q in range(count)
    ]
    barrier = pltpu.get_barrier_semaphore()

    def greet(t, carry):
        pl.semaphore_signal(barrier, inc=1, device_id={"row": lax.rem(row + t, groups)}, device_id_type=MESH)
        pl.semaphore_signal(barrier, inc=1, device_id={"col": lax.rem(col + t, groups)}, device_id_type=MESH)
        return carry

    lax.fori_loop(1, groups, greet, 0)
    inv_load = local(inv.at[0], inv_v, load_sem.at[count])
    cheb_load = local(cheb, cheb_v, load_sem.at[count + 1])
    parity_load = local(parity, parity_v, load_sem.at[count + 3])
    four_loads = []
    for q in range(count):
        part = pl.ds(groups * starts[q] // 2, groups * chunks[q] // 2)
        four_loads.append(local(four.at[:, part], four_v.at[:, part], load_sem.at[count + 4 + q]))
    grads_load = local(grads, grads_v, load_sem.at[count + 2])

    def packed(q):
        return pl.ds(starts[q] * 3 // 2, chunks[q] * 3 // 2)

    def exchange_one(axis, phase, q, t, send, recv):
        me = row if axis == "row" else col
        peer = lax.rem(me + t, groups)
        pltpu.make_async_remote_copy(
            src_ref=send.at[peer, packed(q)],
            dst_ref=recv.at[me, packed(q)],
            send_sem=send_sem.at[phase, q],
            recv_sem=recv_sem.at[phase, q],
            device_id={axis: peer},
            device_id_type=MESH,
        ).start()

    def exchange(axis, phase, q, send, recv):
        def one(t, carry):
            exchange_one(axis, phase, q, t, send, recv)
            return carry

        lax.fori_loop(1, groups, one, 0)
        me = row if axis == "row" else col
        recv[me, packed(q)] = send[me, packed(q)]

    def arrived(phase, q, recv):
        every = recv.at[pl.ds(0, groups - 1), packed(q)]
        pltpu.make_async_copy(every, every, recv_sem.at[phase, q]).wait()

    def sent(phase, q, send):
        every = send.at[pl.ds(0, groups - 1), packed(q)]
        pltpu.make_async_copy(every, every, send_sem.at[phase, q]).wait()

    for half in range(2):
        for c in range(2):
            force[half, c * LANES + SHARE : (c + 1) * LANES, :] = jnp.zeros((LANES - SHARE, half_z), bf16)

    for q in range(count):
        size, at = chunks[q], starts[q]
        adj_loads[q].wait()

        def spread(p, carry, size=size, at=at, q=q):
            blank = jnp.zeros((BATCH, size, LANES - SHARE), bf16)
            some = pl.ds(p * BATCH, BATCH)
            parts = [jnp.concatenate([adj_v[c, some, pl.ds(at, size), :], blank], axis=2) for c in range(2)]
            send_a[some, packed(q)] = pack(*parts)
            return carry

        lax.fori_loop(0, groups // BATCH, spread, 0)
        if q == 0:
            pl.semaphore_wait(barrier, 2 * (groups - 1))
        exchange("row", 0, q, send_a, recv_a)

    def gather(q, recv):
        size = chunks[q]

        def one(s, carry):
            first, second = unpack(recv[pl.ds(s * BATCH, BATCH), packed(q)])
            for c, parts in enumerate((first, second)):
                for quad in range(BATCH // 4):
                    for i, tile in enumerate(close_lanes([parts[4 * quad + i] for i in range(4)])):
                        at = pl.ds(pl.multiple_of(s * (BATCH * SHARE), LANES) + (3 * quad + i) * LANES, LANES)
                        lhs[c * size : (c + 1) * size, at] = tile
            return carry

        lax.fori_loop(0, groups // BATCH, one, 0)

    def post(n, q, value, send):
        size = chunks[q]
        for quad in range(quads):
            tiles = [slice((3 * quad + i) * LANES, (3 * quad + i + 1) * LANES) for i in range(3)]
            first, second = (
                spread_lanes([value[c * size : (c + 1) * size, tile] for tile in tiles]) for c in range(2)
            )
            for j in range(4):
                send[4 * (quads * n + quad) + j, packed(q)] = pack(first[j], second[j])

    def to_points(q):
        size, at = chunks[q], starts[q]
        arrived(0, q, recv_a)
        gather(q, recv_a)
        if q == 0:
            inv_load.wait()

        def solve(n, carry):
            cols = pl.ds(pl.multiple_of(n * tile, tile), tile)
            value = jnp.dot(lhs[0 : 2 * size, :], inv_v[:, cols], preferred_element_type=f32)
            solved[2 * at : 2 * (at + size), cols] = value
            rounded[0 : 2 * size, cols] = value.astype(bf16)
            return carry

        lax.fori_loop(0, length_y // tile, solve, 0)
        if q == 0:
            cheb_load.wait()

        def evaluate(n, carry):
            cols = pl.ds(pl.multiple_of(n * (384 * quads), 384), 384 * quads)
            value = jnp.dot(rounded[0 : 2 * size, :], cheb_v[:, cols], preferred_element_type=f32)
            post(n, q, value.astype(bf16), send_b)
            return carry

        lax.fori_loop(0, groups // (4 * quads), evaluate, 0)
        exchange("col", 1, q, send_b, recv_b)

    def to_physical(q):
        size, at = chunks[q], starts[q]
        depth = groups * size
        arrived(1, q, recv_b)

        def one(s, carry):
            rows = pl.ds(pl.multiple_of(s * (BATCH * size), LANES), BATCH * size)
            for c, part in enumerate(unpack(recv_b[pl.ds(s * BATCH, BATCH), packed(q)])):
                turned[c * LANES : (c + 1) * LANES, rows] = part.reshape(BATCH * size, LANES).T
            return carry

        lax.fori_loop(0, groups // BATCH, one, 0)
        if q == 0:
            parity_load.wait()

        def sort(b, carry):
            cols = pl.ds(pl.multiple_of(b * BLOCK, BLOCK), BLOCK)
            value = jnp.dot(turned[:, cols], parity_v[...], preferred_element_type=f32).astype(bf16)
            half = pl.ds(pl.multiple_of(b * LANES, LANES), LANES)
            for parity in range(2):
                sorted_v[parity, :, half] = value[:, parity * LANES : (parity + 1) * LANES]
            return carry

        lax.fori_loop(0, depth // BLOCK, sort, 0)
        four_loads[q].wait()
        if q == count - 1:
            grads_load.wait()

        def synthesise(start, width):
            cols = pl.ds(start, width)
            rows = slice(groups * at // 2, groups * (at + size) // 2)
            values = []
            for parity in range(2):
                value = jnp.dot(
                    sorted_v[parity, :, 0 : depth // 2], four_v[parity, rows, cols], preferred_element_type=f32
                )
                values.append(value if q == 0 else value + phys[parity, :, cols])
            if q < count - 1:
                for parity in range(2):
                    phys[parity, :, cols] = values[parity]
                return
            forces = []
            for half in range(2):
                value = values[0] + values[1] if half == 0 else values[0] - values[1]
                first, second = value[0:SHARE], value[LANES : LANES + SHARE]
                g = [grads_v[i, 0, :, pl.ds(start + half * half_z, width)].astype(f32) for i in range(4)]
                forces.append((g[0] * first + g[2] * second, g[1] * first + g[3] * second))
            for c in range(2):
                rows = slice(c * LANES, c * LANES + SHARE)
                force[0, rows, cols] = (forces[0][c] + forces[1][c]).astype(bf16)
                force[1, rows, cols] = (forces[0][c] - forces[1][c]).astype(bf16)

        def synthesise_one(n, carry):
            synthesise(pl.multiple_of(n * WIDTH, LANES), WIDTH)
            return carry

        lax.fori_loop(0, half_z // WIDTH, synthesise_one, 0)
        if half_z % WIDTH:
            synthesise(half_z // WIDTH * WIDTH, half_z % WIDTH)

    def analyse(q):
        size, at = chunks[q], starts[q]
        several = BLOCK // size

        def one(n, carry):
            rows = pl.ds(pl.multiple_of(groups * at // 2 + n * BLOCK, BLOCK), BLOCK)
            halves = [
                lax.dot_general(four_v[parity, rows, :], force[parity], NT, preferred_element_type=f32).astype(bf16)
                for parity in range(2)
            ]
            for b in range(2):
                part = slice(b * LANES, (b + 1) * LANES)
                value = jnp.concatenate([halves[0][part], halves[1][part]], axis=0)
                value = jnp.dot(parity_v[...], value, preferred_element_type=f32).astype(bf16)
                for j in range(several):
                    block = value[j * size : (j + 1) * size]
                    letter = pack(block[:, :LANES], block[:, LANES:])
                    send_c[(2 * n + b) * several + j, packed(q)] = letter
            return carry

        lax.fori_loop(0, groups // (2 * several), one, 0)
        exchange("col", 2, q, send_c, recv_c)

    def update(q):
        size, at = chunks[q], starts[q]
        arrived(2, q, recv_c)
        gather(q, recv_c)

        def one(n, carry):
            cols = pl.ds(pl.multiple_of(n * (384 * quads), 384), 384 * quads)
            value = jnp.dot(lhs[0 : 2 * size, :], cheb_v[:, cols], preferred_element_type=f32)
            value = solved[2 * at : 2 * (at + size), cols] + f32(step_weight) * value
            post(n, q, value.astype(bf16), send_d)
            return carry

        lax.fori_loop(0, groups // (4 * quads), one, 0)
        exchange("row", 3, q, send_d, recv_d)

    def finish(q):
        size, at = chunks[q], starts[q]
        arrived(3, q, recv_d)

        def one(s, carry):
            some = pl.ds(s * BATCH, BATCH)
            for c, part in enumerate(unpack(recv_d[some, packed(q)])):
                out_v[c, some, pl.ds(at, size), :] = part[..., :SHARE]
            return carry

        lax.fori_loop(0, groups // BATCH, one, 0)
        return local(out_v.at[:, :, pl.ds(at, size)], out.at[:, :, pl.ds(at, size)], out_sem.at[q])

    for q in range(count):
        to_points(q)
        if 0 < q < count - 1:
            to_physical(q - 1)
    to_physical(count - 2)
    to_physical(count - 1)
    order = list(reversed(range(count)))
    analyse(order[0])
    for q, ahead in zip(order, order[1:] + [None]):
        if ahead is not None:
            analyse(ahead)
        update(q)
    writes = [finish(q) for q in order]
    for q in range(count):
        for phase, send in enumerate((send_a, send_b, send_c, send_d)):
            sent(phase, q, send)
        writes[q].wait()


def on_device(groups, chunks, adjoint_in, solve_inverse, gradient_fields):
    local_modes = adjoint_in.shape[2]
    length_y = solve_inverse.shape[1]
    points_z = gradient_fields.shape[3]
    cheb = jnp.asarray(cheb_build(length_y))
    parity = jnp.asarray(parity_build())
    four = jnp.asarray(fourier_build(local_modes * groups, points_z, groups, chunks))
    f32, bf16 = jnp.float32, jnp.bfloat16
    most = max(chunks)
    count = len(chunks)
    mail = pltpu.VMEM((groups, local_modes * 3 // 2, LANES), bf16)
    result = pl.pallas_call(
        functools.partial(kernel, chunks),
        out_shape=jax.ShapeDtypeStruct(adjoint_in.shape, bf16),
        in_specs=[pl.BlockSpec(memory_space=pl.ANY)] * 6,
        out_specs=pl.BlockSpec(memory_space=pl.ANY),
        scratch_shapes=[
            pltpu.VMEM(adjoint_in.shape, bf16),
            pltpu.VMEM(solve_inverse.shape[1:], bf16),
            pltpu.VMEM(gradient_fields.shape, bf16),
            pltpu.VMEM(cheb.shape, bf16),
            pltpu.VMEM(four.shape, bf16),
            pltpu.VMEM(parity.shape, bf16),
            *[mail] * 8,
            pltpu.VMEM((2 * most, length_y), bf16),
            pltpu.VMEM((2 * local_modes, length_y), f32),
            pltpu.VMEM((2 * most, length_y), bf16),
            pltpu.VMEM((2 * LANES, groups * most), bf16),
            pltpu.VMEM((2, 2 * LANES, groups * most // 2), bf16),
            pltpu.VMEM((2, 2 * LANES, points_z // 2), f32),
            pltpu.VMEM((2, 2 * LANES, points_z // 2), bf16),
            pltpu.VMEM(adjoint_in.shape, bf16),
            pltpu.SemaphoreType.DMA((2 * count + 4,)),
            pltpu.SemaphoreType.DMA((4, count)),
            pltpu.SemaphoreType.DMA((4, count)),
            pltpu.SemaphoreType.DMA((count,)),
        ],
        compiler_params=pltpu.CompilerParams(
            collective_id=0, has_side_effects=True, vmem_limit_bytes=VMEM_LIMIT
        ),
        cost_estimate=pl.CostEstimate(flops=12_000_000_000, bytes_accessed=40_000_000, transcendentals=0),
    )(adjoint_in, solve_inverse, gradient_fields, cheb, four, parity)
    return result.astype(f32)


def solution(mesh):
    groups = mesh.shape["row"]
    return jax.shard_map(
        functools.partial(on_device, groups, CHUNKS),
        mesh=mesh,
        in_specs=(P(None, None, "col", "row"), P("row", None, None), P(None, "row", "col", None)),
        out_specs=P(None, None, "col", "row"),
        check_vma=False,
    )
```

time: 140 us -> 86.2 us (0.62)
  Pallas kernels: 137 us -> 82.2 us
    pallas_call x1, Pallas kernels: 137 us -> 82.2 us  [on_device(): pl.pallas_call(functools.partial(kernel, chunks), out_shape=jax.ShapeDtyp...]
where the time goes in v3:
time: 86.2 us; the launch traced here: 85.4 us
  Pallas kernels  82.2 us (95%)
  other arithmetic  3.12 us (4%)
    pallas_call x1, Pallas kernels, on_device(): pl.pallas_call(functools.partial(kernel, chunks), out_shape=jax.ShapeDtyp...  82.2 us
    convert_element_type x1, other arithmetic, on_device(): return result.astype(f32)  3.12 us

profile of v3, /device:TPU:1, one launch (start us, length us, event | category | flops | bytes accessed | tf_op | source)
XLA Modules:
  0.0 85.4 jit_solution(9681816062286778965)
XLA Ops:
  0.0 82.2 %shard_map.64 = bf16[2,16,160,96]{3,2,1,0:T(8,128)(2,1)} custom-call(bf16[2,16,160,96]{3,2,1,0:T(8,128)(2,1)} %adj.1, bf16[1,1536,1536]{2,1,0:T(8,128)(2,1)} %inv.1, bf16[4,1,96,3840]{3,2,1,0:T(8,128)(2,1)} %grads.1, bf16[1536,1536]{1,0:T(8,128)(2,1)} %constant.6.clone.cheb, bf16[2,1280,1920]{2,1,0:T(8,128)(2,1)} %constant.8.clone.four, ...), custom_call_target="tpu_custom_call" | custom-call | flops 12000000000 | bytes 40000000 | tf_op jit(solution)/shard_map/pallas_call | solution.py:393
  82.2 3.1 %convert_element_type.3 = f32[2,16,160,96]{3,2,1,0:T(8,128)} convert(bf16[2,16,160,96]{3,2,1,0:T(8,128)(2,1)} %shard_map.64) | non-fusion elementwise | flops 491520 | bytes 2949120 | tf_op jit(solution)/shard_map/convert_element_type | solution.py:424

commit v4 on v3

--- a/solution.py
+++ b/solution.py
@@ -20,7 +20,7 @@
 BLOCK = 256
 BATCH = 16
 SHARE = 96
-CHUNKS = (64, 64, 32)
+CHUNKS = (64, 32, 32, 32)
 SOLVE_TILE = 768
 POST = 4
 WIDTH = 640
@@ -362,15 +362,12 @@
 
     for q in range(count):
         to_points(q)
-        if 0 < q < count - 1:
-            to_physical(q - 1)
-    to_physical(count - 2)
-    to_physical(count - 1)
+    for q in range(count):
+        to_physical(q)
     order = list(reversed(range(count)))
-    analyse(order[0])
-    for q, ahead in zip(order, order[1:] + [None]):
-        if ahead is not None:
-            analyse(ahead)
+    for q in order:
+        analyse(q)
+    for q in order:
         update(q)
     writes = [finish(q) for q in order]
     for q in range(count):

time: 86.2 us -> 84.6 us (0.981)
  no operation moved by 1% of the time
where the time goes in v4:
time: 84.6 us; the launch traced here: 84.5 us
  Pallas kernels  81.4 us (96%)
  other arithmetic  3.12 us (4%)
    pallas_call x1, Pallas kernels, on_device(): pl.pallas_call(functools.partial(kernel, chunks), out_shape=jax.ShapeDtyp...  81.4 us
    convert_element_type x1, other arithmetic, on_device(): return result.astype(f32)  3.12 us

profile of v4, /device:TPU:1, one launch (start us, length us, event | category | flops | bytes accessed | tf_op | source)
XLA Modules:
  0.0 84.5 jit_solution(1787832203441779394)
XLA Ops:
  0.0 81.4 %shard_map.64 = bf16[2,16,160,96]{3,2,1,0:T(8,128)(2,1)} custom-call(bf16[2,16,160,96]{3,2,1,0:T(8,128)(2,1)} %adj.1, bf16[1,1536,1536]{2,1,0:T(8,128)(2,1)} %inv.1, bf16[4,1,96,3840]{3,2,1,0:T(8,128)(2,1)} %grads.1, bf16[1536,1536]{1,0:T(8,128)(2,1)} %constant.6.clone.cheb, bf16[2,1280,1920]{2,1,0:T(8,128)(2,1)} %constant.8.clone.four, ...), custom_call_target="tpu_custom_call" | custom-call | flops 12000000000 | bytes 40000000 | tf_op jit(solution)/shard_map/pallas_call | solution.py:390
  81.4 3.1 %convert_element_type.3 = f32[2,16,160,96]{3,2,1,0:T(8,128)} convert(bf16[2,16,160,96]{3,2,1,0:T(8,128)(2,1)} %shard_map.64) | non-fusion elementwise | flops 491520 | bytes 2949120 | tf_op jit(solution)/shard_map/convert_element_type | solution.py:421

commit v5 on v4

--- a/solution.py
+++ b/solution.py
@@ -137,15 +137,6 @@
         return carry
 
     lax.fori_loop(1, groups, greet, 0)
-    inv_load = local(inv.at[0], inv_v, load_sem.at[count])
-    cheb_load = local(cheb, cheb_v, load_sem.at[count + 1])
-    parity_load = local(parity, parity_v, load_sem.at[count + 3])
-    four_loads = []
-    for q in range(count):
-        part = pl.ds(groups * starts[q] // 2, groups * chunks[q] // 2)
-        four_loads.append(local(four.at[:, part], four_v.at[:, part], load_sem.at[count + 4 + q]))
-    grads_load = local(grads, grads_v, load_sem.at[count + 2])
-
     def packed(q):
         return pl.ds(starts[q] * 3 // 2, chunks[q] * 3 // 2)
 
@@ -178,9 +169,11 @@
         every = send.at[pl.ds(0, groups - 1), packed(q)]
         pltpu.make_async_copy(every, every, send_sem.at[phase, q]).wait()
 
-    for half in range(2):
-        for c in range(2):
-            force[half, c * LANES + SHARE : (c + 1) * LANES, :] = jnp.zeros((LANES - SHARE, half_z), bf16)
+    def clear(t, carry):
+        for half in range(2):
+            for c in range(2):
+                force[half, c * LANES + SHARE : (c + 1) * LANES, :] = jnp.zeros((LANES - SHARE, half_z), bf16)
+        return carry
 
     for q in range(count):
         size, at = chunks[q], starts[q]
@@ -195,8 +188,18 @@
 
         lax.fori_loop(0, groups // BATCH, spread, 0)
         if q == 0:
+            lax.fori_loop(0, 1, clear, 0)
             pl.semaphore_wait(barrier, 2 * (groups - 1))
         exchange("row", 0, q, send_a, recv_a)
+
+    inv_load = local(inv.at[0], inv_v, load_sem.at[count])
+    cheb_load = local(cheb, cheb_v, load_sem.at[count + 1])
+    parity_load = local(parity, parity_v, load_sem.at[count + 3])
+    four_loads = []
+    for q in range(count):
+        part = pl.ds(groups * starts[q] // 2, groups * chunks[q] // 2)
+        four_loads.append(local(four.at[:, part], four_v.at[:, part], load_sem.at[count + 4 + q]))
+    grads_load = local(grads, grads_v, load_sem.at[count + 2])
 
     def gather(q, recv):
         size = chunks[q]

time: 84.6 us -> 84.7 us (level)
  no operation moved by 1% of the time
where the time goes in v5:
time: 84.7 us; the launch traced here: 84.6 us
  Pallas kernels  81.4 us (96%)
  other arithmetic  3.12 us (4%)
    pallas_call x1, Pallas kernels, on_device(): pl.pallas_call(functools.partial(kernel, chunks), out_shape=jax.ShapeDtyp...  81.4 us
    convert_element_type x1, other arithmetic, on_device(): return result.astype(f32)  3.12 us

profile of v5, /device:TPU:1, one launch (start us, length us, event | category | flops | bytes accessed | tf_op | source)
XLA Modules:
  0.0 84.6 jit_solution(11269200983598386619)
XLA Ops:
  0.0 81.4 %shard_map.64 = bf16[2,16,160,96]{3,2,1,0:T(8,128)(2,1)} custom-call(bf16[2,16,160,96]{3,2,1,0:T(8,128)(2,1)} %adj.1, bf16[1,1536,1536]{2,1,0:T(8,128)(2,1)} %inv.1, bf16[4,1,96,3840]{3,2,1,0:T(8,128)(2,1)} %grads.1, bf16[1536,1536]{1,0:T(8,128)(2,1)} %constant.6.clone.cheb, bf16[2,1280,1920]{2,1,0:T(8,128)(2,1)} %constant.8.clone.four, ...), custom_call_target="tpu_custom_call" | custom-call | flops 12000000000 | bytes 40000000 | tf_op jit(solution)/shard_map/pallas_call | solution.py:393
  81.4 3.1 %convert_element_type.3 = f32[2,16,160,96]{3,2,1,0:T(8,128)} convert(bf16[2,16,160,96]{3,2,1,0:T(8,128)(2,1)} %shard_map.64) | non-fusion elementwise | flops 491520 | bytes 2949120 | tf_op jit(solution)/shard_map/convert_element_type | solution.py:424
